TPU v7x, 32 devices: a whole 2x2x4 slice. The times are simulated.
32 devices in a mesh: batch: 2 (over y), freq: 8 (over z, x), elem: 2 (over core).
Axes of the slice: x: 2, y: 2, z: 4, core: 2. Of those that a mesh axis runs over, the one named last changes fastest.
Arguments:
- flaw_cells: int32 [512], P('batch'), parts along dimension 0, may hold values from 0 to 255, each once
- flaw_blocks: int32 [16], P('batch'), parts along dimension 0, may hold values from 0 to 7, each once
- element_channel: int32 [256], P('elem'), may hold values from 0 to 255, each once
- focal_delay: float32 [256, 256], replicated, may hold values from 0 to 64
- beam_field: bfloat16 [128, 2, 256, 256], P('freq', None, 'elem'), may hold values from -0.125 to 0.125
- flaw_size: float32 [4, 128], P('batch'), parts along dimension 0, may hold values from 0.5 to 4
- flaw_slope: float32 [4, 128], P('batch'), parts along dimension 0, may hold values from 0.2 to 1
- noise_level: float32 [4, 128], P(('batch', 'elem'), 'freq'), parts along dimension 0, may hold values from 0.5 to 5
Outputs:
- flaw_peak: float32 [4, 128], P(('batch', 'elem'), 'freq'), parts along dimension 0
- detection: float32 [4, 128], P(('batch', 'elem'), 'freq'), parts along dimension 0
There are 2 independent parts, one for each index of `batch`. A program takes and returns all parts, laid end to end along the dimension named above; an argument that names none is the same for every part. Nothing has to cross between parts.
Inputs may be any that keep to these rules, and one draw needn't show every extreme that they name: `flaw_cells`: every site holds exactly one flaw. `flaw_blocks`: every scan block belongs to exactly one flaw group. `element_channel`: every channel drives exactly one element.
All inputs are finite; a program needn't handle non-finite values.
Results may differ from a plain program's by a relative error of at most 0.0011.
Values may be sent and summed in bfloat16 or wider, within the bound.
No kernel may reach another device: no remote copies, remote signals or barrier semaphores. Data moves between devices by JAX's collectives and lax.ppermute only.
A program may use at most 64 MiB of HBM per device.

v0:
```python
import functools
import math

import jax
import jax.numpy as jnp
from jax import lax
from jax.experimental import pallas as pl
from jax.experimental.pallas import tpu as pltpu
from jax.sharding import PartitionSpec as P

W_DEV = 16
W_HALF = W_DEV // 2
FG = 128
NB = 4
SB = 32
T_CAP = 1024

EDGE = 0.6
STEEP = 3.0
EPS = 1e-05

ROWS = NB * SB
VMEM_BYTES = 48 * 1024 * 1024


def sin_half_turn(turns):
    angle = turns * math.pi
    square = angle * angle
    sine = 1.0 / 6227020800.0
    for factorial in (-39916800.0, 362880.0, -5040.0, 120.0, -6.0, 1.0):
        sine = sine * square + 1.0 / factorial
    cosine = 1.0 / 479001600.0
    for factorial in (-3628800.0, 40320.0, -720.0, 24.0, -2.0, 1.0):
        cosine = cosine * square + 1.0 / factorial
    return sine * angle, cosine


def sincos_turns(turns):
    rest = turns - jnp.floor(turns + 0.5)
    sine, cosine = sin_half_turn(rest)
    return 2.0 * sine * cosine, 1.0 - 2.0 * sine * sine


def dot(left, right, contract):
    return lax.dot_general(
        left, right, (contract, ((), ())), preferred_element_type=jnp.float32
    )


def slot_order(slots):
    row = lax.broadcasted_iota(jnp.int32, (FG, FG), 0)
    column = lax.broadcasted_iota(jnp.int32, (FG, FG), 1)
    if slots > 1:
        row = row ^ (lax.axis_index("freq") * (FG // slots))
    return row == column


def delay_pieces(channel_ref, delay_ref, elements):
    channel_sel = (
        (
            lax.broadcasted_iota(jnp.int32, (delay_ref.shape[0], elements), 0)
            == channel_ref[...]
        )
        .astype(jnp.float32)
        .T.astype(jnp.bfloat16)
    )
    rest = delay_ref[...]
    pieces = []
    for _ in range(3):
        piece = rest.astype(jnp.bfloat16)
        rest = rest - piece.astype(jnp.float32)
        pieces.append(dot(channel_sel, piece, ((1,), (0,))).astype(jnp.bfloat16))
    return pieces


def turned(law, step):
    return law[0] * step[0] - law[1] * step[1], law[1] * step[0] + law[0] * step[1]


def prepare(freq_total, slots, which, pieces, cells_ref, size_ref, slope_ref, blocks_ref):
    sites = cells_ref.shape[1]
    first_freq = lax.axis_index("freq") * W_DEV
    order = slot_order(slots)
    cells = jnp.where(which == 0, cells_ref[:, :FG], cells_ref[:, FG:])
    cell_sel = lax.broadcasted_iota(jnp.int32, (sites, FG), 0) == cells
    pick = dot(
        order.astype(jnp.bfloat16), cell_sel.astype(jnp.bfloat16), ((1,), (1,))
    ).astype(jnp.bfloat16)
    size = size_ref[pl.ds(which, 1), :]
    turn = size * slope_ref[pl.ds(which, 1), :] * (1.0 / freq_total)
    size = jnp.sum(jnp.where(order, size, 0.0), axis=1, keepdims=True)
    turn = jnp.sum(jnp.where(order, turn, 0.0), axis=1, keepdims=True)
    freq = first_freq + lax.broadcasted_iota(jnp.int32, (FG, FG), 1)
    sine, cosine = sincos_turns(turn * freq.astype(jnp.float32))
    k_real = size * (1.0 + EDGE) * cosine
    k_imag = size * (EDGE - 1.0) * sine
    lane = lax.broadcasted_iota(jnp.int32, (1, ROWS), 1)
    position = lane & (SB - 1)
    for j in range(NB):
        block = blocks_ref[which * NB + j]
        position = position + jnp.where((lane >> 5) == j, block * SB, 0)
    scan_sel = (
        lax.broadcasted_iota(jnp.int32, (pieces[0].shape[1], ROWS), 0) == position
    ).astype(jnp.bfloat16)
    delays = None
    for piece in pieces:
        moved = dot(piece, scan_sel, ((1,), (0,)))
        delays = moved if delays is None else delays + moved
    phase = delays * (0.5 / freq_total)
    unit = sincos_turns(phase)[::-1]
    base = sincos_turns(phase * first_freq.astype(jnp.float32))[::-1]
    return *base, *turned(unit, unit), *turned(base, unit), pick, k_real, k_imag


def partial_spectra(parity, law, step, pick, k_real, k_imag, field_ref, wait, out_ref, scratch):
    picked_ref, law_ref, rows_ref = scratch
    elements, sites = field_ref.shape[3:]
    for w in range(W_HALF):
        c = law[0].astype(jnp.bfloat16)
        s = law[1].astype(jnp.bfloat16)
        law_ref[w, :elements, :ROWS] = c
        law_ref[w, :elements, ROWS:] = -s
        law_ref[w, elements:, :ROWS] = s
        law_ref[w, elements:, ROWS:] = c
        if w < W_HALF - 1:
            law = turned(law, step)
    for w in range(W_HALF):
        wait(w)
        picked_ref[w] = dot(
            pick, field_ref[w, parity].reshape(2 * elements, sites), ((1,), (1,))
        ).astype(jnp.bfloat16)
    for w in range(W_HALF):
        product = dot(picked_ref[w], law_ref[w], ((1,), (0,)))
        real_part = product[:, :ROWS]
        imag_part = product[:, ROWS:]
        kr = k_real[:, 2 * w + parity : 2 * w + parity + 1]
        ki = k_imag[:, 2 * w + parity : 2 * w + parity + 1]
        rows_ref[pl.ds(2 * w, FG, stride=W_DEV), :] = kr * real_part - ki * imag_part
        rows_ref[pl.ds(2 * w + 1, FG, stride=W_DEV), :] = kr * imag_part + ki * real_part
    out_ref[...] = rows_ref[...].reshape(FG, W_DEV, ROWS).astype(jnp.bfloat16)


def even_spectra(values, field_ref, wait, out_ref, kept, scratch):
    for ref, value in zip(kept, values[2:]):
        ref[...] = value
    partial_spectra(
        0, values[:2], values[2:4], *values[6:], field_ref, wait, out_ref, scratch
    )


def other_even_kernel(freq_total, slots, *refs):
    field_hbm, *small_hbm = refs[:7]
    out_ref, field_ref, cells_ref, size_ref, slope_ref, pieces_ref, *kept = refs[7:20]
    channel_ref, delay_ref, blocks_ref, field_sem, small_sem, *scratch = refs[20:]
    small = (cells_ref, size_ref, slope_ref, channel_ref, delay_ref, blocks_ref)
    copies = [
        pltpu.make_async_copy(source, target, small_sem.at[i])
        for i, (source, target) in enumerate(zip(small_hbm, small))
    ]
    for copy in copies:
        copy.start()
    part = W_HALF // 2
    field_copies = [
        pltpu.make_async_copy(
            field_hbm.at[pl.ds(i * part, part), parity],
            field_ref.at[pl.ds(i * part, part), parity],
            field_sem.at[parity, i],
        )
        for parity in range(2)
        for i in range(2)
    ]
    for copy in field_copies:
        copy.start()
    for copy in copies:
        copy.wait()
    pieces = delay_pieces(channel_ref, delay_ref, field_ref.shape[3])
    for i, piece in enumerate(pieces):
        pieces_ref[i] = piece
    other = 1 - lax.axis_index("elem")
    values = prepare(
        freq_total, slots, other, pieces, cells_ref, size_ref, slope_ref, blocks_ref
    )

    def wait(w):
        if w % part == 0:
            field_copies[w // part].wait()

    even_spectra(values, field_ref, wait, out_ref, kept, scratch)
    for copy in field_copies[2:]:
        copy.wait()


def own_even_kernel(freq_total, slots, field_ref, cells_ref, size_ref, slope_ref, *refs):
    pieces_ref, blocks_ref, out_ref, *refs = refs
    kept, scratch = refs[:7], refs[7:]
    pieces = [pieces_ref[i] for i in range(pieces_ref.shape[0])]
    group = lax.axis_index("elem")
    values = prepare(
        freq_total, slots, group, pieces, cells_ref, size_ref, slope_ref, blocks_ref
    )
    even_spectra(values, field_ref, lambda w: None, out_ref, kept, scratch)


def odd_kernel(after, field_ref, *refs):
    step, law, pick = refs[0:2], refs[2:4], refs[4]
    k_refs, (out_ref, *scratch) = refs[5:7], refs[7 + after :]
    partial_spectra(
        1,
        [ref[...] for ref in law],
        [ref[...] for ref in step],
        pick[...],
        *k_refs,
        field_ref,
        lambda w: None,
        out_ref,
        scratch,
    )


def call(kernel, name, in_specs, out_shape, scratch):
    vmem = pl.BlockSpec(memory_space=pltpu.VMEM)
    return pl.pallas_call(
        kernel,
        in_specs=in_specs,
        out_specs=[vmem] * len(out_shape),
        out_shape=out_shape,
        scratch_shapes=scratch,
        compiler_params=pltpu.CompilerParams(vmem_limit_bytes=VMEM_BYTES),
        cost_estimate=pl.CostEstimate(flops=1000, bytes_accessed=1000, transcendentals=0),
        name=name,
    )


def even_partials(field, small, swap, freq_total, slots):
    elements, sites = field.shape[3:]
    vmem = pl.BlockSpec(memory_space=pltpu.VMEM)
    hbm = pl.BlockSpec(memory_space=pltpu.HBM)
    smem = pl.BlockSpec(memory_space=pltpu.SMEM)
    cells, length, slope, channel, delay, blocks = small
    pinned = [pltpu.with_memory_space_constraint(a, pltpu.HBM) for a in (field, *small)]
    work = [
        pltpu.VMEM((W_HALF, FG, 2 * elements), jnp.bfloat16),
        pltpu.VMEM((W_HALF, 2 * elements, 2 * ROWS), jnp.bfloat16),
        pltpu.VMEM((FG * W_DEV, ROWS), jnp.float32),
    ]
    out = jax.ShapeDtypeStruct((FG, W_DEV, ROWS), jnp.bfloat16)
    pieces = jax.ShapeDtypeStruct((3, elements, delay.shape[1]), jnp.bfloat16)
    kept = [jax.ShapeDtypeStruct((elements, ROWS), jnp.float32)] * 4
    kept += [jax.ShapeDtypeStruct((FG, sites), jnp.bfloat16)]
    kept += [jax.ShapeDtypeStruct((FG, FG), jnp.float32)] * 2
    copied = [jax.ShapeDtypeStruct(a.shape, a.dtype) for a in (field, cells, length, slope)]
    other, field, cells, length, slope, pieces, *other_kept = call(
        functools.partial(other_even_kernel, freq_total, slots),
        "other_even",
        [hbm] * len(pinned),
        [out, *copied, pieces, *kept],
        [
            pltpu.VMEM(channel.shape, channel.dtype),
            pltpu.VMEM(delay.shape, delay.dtype),
            pltpu.SMEM(blocks.shape, blocks.dtype),
            pltpu.SemaphoreType.DMA((2, 2)),
            pltpu.SemaphoreType.DMA((len(small),)),
            *work,
        ],
    )(*pinned)
    moved = lax.ppermute(other, "elem", swap)
    own, *own_kept = call(
        functools.partial(own_even_kernel, freq_total, slots),
        "own_even",
        [vmem] * 5 + [smem],
        [out, *kept],
        work,
    )(field, cells, length, slope, pieces, blocks)

    def odd_partials(*after):
        other, own = (
            call(
                functools.partial(odd_kernel, len(first)),
                name,
                [vmem] * 8 + [pl.BlockSpec(memory_space=pl.ANY)] * len(first),
                [out],
                work,
            )(field, *kept, *first)[0]
            for name, kept, first in (
                ("other_odd", other_kept, ()),
                ("own_odd", own_kept, after),
            )
        )
        return own, lax.ppermute(other, "elem", swap)

    return own, moved, odd_partials


def total(own_ref, moved_ref, rows):
    both = own_ref[rows].astype(jnp.float32) + moved_ref[rows].astype(jnp.float32)
    return both.astype(jnp.bfloat16)


def add_even_kernel(size, early, own_ref, moved_ref, held_ref, *refs):
    slots = range(own_ref.shape[0] // size)
    for slot, ref in zip(early, refs):
        ref[...] = total(own_ref, moved_ref, pl.ds(slot * size, size))
    for i, slot in enumerate([s for s in slots if s not in early]):
        held_ref[pl.ds(i * size, size)] = total(own_ref, moved_ref, pl.ds(slot * size, size))


def add_even(own, moved, size, early):
    vmem = pl.BlockSpec(memory_space=pltpu.VMEM)
    flaws, planes, rows = own.shape
    shapes = [jax.ShapeDtypeStruct((flaws - size * len(early), planes, rows), own.dtype)]
    shapes += [jax.ShapeDtypeStruct((size, planes, rows), own.dtype)] * len(early)
    return call(
        functools.partial(add_even_kernel, size, early), "add_even", [vmem] * 2, shapes, []
    )(own, moved)


def add_odd_kernel(size, early, late, own_ref, moved_ref, held_ref, *refs):
    planes = own_ref.shape[1]
    held = sorted(late)
    for slot, ref in zip((*early, *late), refs):
        value = total(own_ref, moved_ref, pl.ds(slot * size, size))
        if slot in early:
            ref[...] = value
        else:
            ref[:, :planes] = held_ref[pl.ds(held.index(slot) * size, size)]
            ref[:, planes:] = value


def add_odd(own, moved, held, size, early, late):
    vmem = pl.BlockSpec(memory_space=pltpu.VMEM)
    _, planes, rows = own.shape
    shapes = [
        jax.ShapeDtypeStruct((size, planes * (1 if slot in early else 2), rows), own.dtype)
        for slot in (*early, *late)
    ]
    return call(
        functools.partial(add_odd_kernel, size, early, late), "add_odd", [vmem] * 3, shapes, []
    )(own, moved, held)


def table_kernel(freq_total, slots, table_ref):
    height, depth = table_ref.shape[2:]
    time_block = height // 2
    row = lax.broadcasted_iota(jnp.int32, (height, depth // 2), 0)
    column = lax.broadcasted_iota(jnp.int32, (height, depth // 2), 1)
    out_imag = (row >= time_block).astype(jnp.int32)
    time = pl.program_id(0) * time_block + row - out_imag * time_block
    for parity in range(2):
        freq = (column >> 1) * 2 + parity
        if slots > 1:
            freq = freq ^ (lax.axis_index("freq") * W_DEV)
        steps = freq * time + ((column & 1) - out_imag) * (freq_total // 2)
        steps = (steps + 2 * freq_total) & (2 * freq_total - 1)
        _, value = sincos_turns(steps.astype(jnp.float32) * (0.5 / freq_total))
        high = value.astype(jnp.bfloat16)
        table_ref[0, parity, :, : depth // 2] = high
        table_ref[0, parity, :, depth // 2 :] = (
            value - high.astype(jnp.float32)
        ).astype(jnp.bfloat16)


def table(freq_total, slots, times, time_block):
    blocks = times // time_block
    shape = (blocks, 2, 2 * time_block, 2 * freq_total)
    return pl.pallas_call(
        functools.partial(table_kernel, freq_total, slots),
        grid=(blocks,),
        out_specs=pl.BlockSpec((1, *shape[1:]), lambda i: (i, 0, 0, 0)),
        out_shape=jax.ShapeDtypeStruct(shape, jnp.bfloat16),
        compiler_params=pltpu.CompilerParams(vmem_limit_bytes=VMEM_BYTES),
        name="table",
    )()


def peak_kernel(freq_total, folded, sources, *refs):
    count = len(refs) - 5
    table_ref, noise_ref, peak_ref, found_ref, best_ref = refs[count:]
    step = pl.program_id(0)
    columns = peak_ref.shape[1]
    time_block = table_ref.shape[2] // 2

    @pl.when(step == 0)
    def _():
        best_ref[...] = jnp.zeros_like(best_ref)

    width = min(2, columns)
    for first in range(0, columns, width):
        parts = []
        for parity in range(2):
            spectra = jnp.concatenate(
                [
                    jnp.concatenate(
                        [
                            refs[i][row + first + k, plane : plane + W_DEV, :]
                            for i, row, plane in sources[parity]
                        ]
                        * 2,
                        axis=0,
                    )
                    for k in range(width)
                ],
                axis=1,
            )
            parts.append(dot(table_ref[0, parity], spectra, ((1,), (0,))))
        powers = []
        for signal in [parts[0] + parts[1]] + [parts[0] - parts[1]] * folded:
            real_part = signal[:time_block]
            imag_part = signal[time_block:]
            powers.append(real_part * real_part + imag_part * imag_part)
        power = jnp.maximum(powers[0], powers[-1]) if folded else powers[0]
        power = jnp.max(power, axis=0, keepdims=True)
        for k in range(width):
            row = pl.ds(first + k, 1)
            best_ref[row, :] = jnp.maximum(
                best_ref[row, :], power[:, k * ROWS : (k + 1) * ROWS]
            )

    @pl.when(step == pl.num_programs(0) - 1)
    def _():
        largest = jnp.max(best_ref[...], axis=1, keepdims=True)
        shape = best_ref.shape
        diagonal = lax.broadcasted_iota(jnp.int32, shape, 0) == lax.broadcasted_iota(
            jnp.int32, shape, 1
        )
        largest = jnp.max(jnp.where(diagonal, largest, 0.0), axis=0, keepdims=True)
        peak = jnp.sqrt(largest[:, :columns]) * (1.0 / math.sqrt(freq_total))
        score = STEEP * (jnp.log(peak + EPS) - jnp.log(noise_ref[...]))
        peak_ref[...] = peak
        found_ref[...] = 1.0 / (1.0 + jnp.exp(-score))


def peaks(spectra, sources, twiddles, noise_level, freq_total, folded):
    columns = noise_level.shape[1]
    out_spec = pl.BlockSpec((1, columns), lambda i: (0, 0))
    return pl.pallas_call(
        functools.partial(peak_kernel, freq_total, folded, sources),
        grid=(twiddles.shape[0],),
        in_specs=[pl.BlockSpec(a.shape, lambda i: (0, 0, 0)) for a in spectra]
        + [pl.BlockSpec((1, *twiddles.shape[1:]), lambda i: (i, 0, 0, 0)), out_spec],
        out_specs=[out_spec, out_spec],
        out_shape=[jax.ShapeDtypeStruct((1, columns), jnp.float32)] * 2,
        scratch_shapes=[pltpu.VMEM((max(8, columns), ROWS), jnp.float32)],
        compiler_params=pltpu.CompilerParams(vmem_limit_bytes=VMEM_BYTES),
        name="peaks",
    )(*spectra, twiddles, noise_level)


def body(
    flaw_cells,
    flaw_blocks,
    element_channel,
    focal_delay,
    beam_field,
    flaw_size,
    flaw_slope,
    noise_level,
):
    freq_count = lax.axis_size("freq")
    freq_total = W_DEV * freq_count
    sample_count = min(T_CAP, 2 * freq_total)
    swap = [(0, 1), (1, 0)]
    direct = freq_count == 8
    slots = freq_count if direct else 1
    small = (
        flaw_cells.reshape(1, -1),
        flaw_size,
        flaw_slope,
        element_channel.reshape(1, -1),
        focal_delay,
        flaw_blocks,
    )
    folded = sample_count == 2 * freq_total
    times = sample_count // 2 if folded else sample_count
    twiddles = table(freq_total, slots, times, min(128, times))
    field = beam_field.reshape(W_HALF, 2, *beam_field.shape[1:])
    own, moved, odd_partials = even_partials(field, small, swap, freq_total, slots)
    size = FG // slots
    if direct:

        def send(array, mask):
            pairs = [(a, a ^ mask) for a in range(slots)]
            return lax.ppermute(array, "freq", pairs)

        half = slots // 2
        early = tuple(range(half, half + 2))
        late = (*range(half + 2, slots), *range(2, half), 1, 0)
        held, *sent = add_even(own, moved, size, early)
        even = [send(array, slot) for slot, array in zip(early, sent)]
        own, moved = odd_partials(held)
        sent = add_odd(own, moved, held, size, early, late)
        odd = [send(array, slot) for slot, array in zip(early, sent)]
        sent = dict(zip(late, sent[len(early) :]))
        wide = {slot: send(array, slot) if slot else array for slot, array in sent.items()}
        spectra = [*even, *(wide[s] for s in late if s >= half), *odd]
        spectra += [wide[s] for s in late if s < half]
        place = {id(array): i for i, array in enumerate(spectra)}
        sources = [
            [
                (place[id(some[slot - half])], 0, 0) if slot in early else (place[id(wide[slot])], 0, plane)
                for slot in range(slots)
            ]
            for some, plane in ((even, 0), (odd, W_DEV))
        ]
    else:
        (held,) = add_even(own, moved, size, ())
        own, moved = odd_partials()
        (whole,) = add_odd(own, moved, held, size, (), (0,))
        spectra = [
            lax.all_to_all(whole, "freq", split_axis=0, concat_axis=0, tiled=True)
        ]
        columns = FG // freq_count
        sources = [
            [(0, s * columns, plane) for s in range(freq_count)] for plane in (0, W_DEV)
        ]
    return tuple(peaks(spectra, sources, twiddles, noise_level, freq_total, folded))


def solution(mesh):
    in_specs = (
        P("batch"),
        P("batch"),
        P("elem"),
        P(),
        P("freq", None, "elem", None),
        P("batch", None),
        P("batch", None),
        P(("batch", "elem"), "freq"),
    )
    out_specs = (P(("batch", "elem"), "freq"), P(("batch", "elem"), "freq"))
    return jax.shard_map(body, mesh=mesh, in_specs=in_specs, out_specs=out_specs, check_vma=False)
```

profile of v0, /device:TPU:17, one launch (start us, length us, event | category | flops | bytes accessed | tf_op | source)
XLA Modules:
  0.0 40.6 jit_solution(1433480353949792125)
XLA Ops:
  0.6 3.2 %other_even.1 = (bf16[128,16,128]{2,1,0:T(8,128)(2,1)S(1)}, bf16[8,2,2,128,256]{4,3,2,1,0:T(8,128)(2,1)S(1)}, s32[1,256]{1,0:T(1,128)S(1)}, f32[2,128]{1,0:T(2,1...) custom-call(bf16[8,2,2,128,256]{4,3,2,1,0:T(8,128)(2,1)} %bitcast.3,, ...), custom_call_target="tpu_custom_call" | custom-call | flops 1000 | bytes 1000 | tf_op jit(solution)/shard_map/other_even/pallas_call | solution.py:252
  3.9 0.0 copy-start
  3.9 0.7 %collective-permute-start = (bf16[128,16,128]{2,1,0:T(8,128)(2,1)S(1)}, bf16[128,16,128]{2,1,0:T(8,128)(2,1)S(1)}, u32[]{:S(2)}, u32[]{:S(2)}) collective-permute-start(bf16[128,16,128]{2,1,0:T(8,128)(2,1)S(1)} %get-tuple-element.40), channel_id=1, source_target_pairs={{0,1},{1,0},{2,3},{3,2},{4,5},{5,4},{6,7},{7,6},{8,9},{9,8},{10,11... | collective-permute-start | bytes 1572872 | tf_op jit(solution)/shard_map/ppermute | solution.py:266
  4.6 0.9 %other_odd.1 = bf16[128,16,128]{2,1,0:T(8,128)(2,1)S(1)} custom-call(bf16[8,2,2,128,256]{4,3,2,1,0:T(8,128)(2,1)S(1)} %get-tuple-element.34.field_ref, f32[128,128]{1,0:T(8,128)S(1)} %get-tuple-element.51.refs_0_, f32[128,128]{1,0:T(8,128)S(1)} %get-tuple-element.52.refs_1_, f32[128,128]{1,0:T(8,128)S(1)} %get-tuple-element.53.refs_2_, ...), custom_call_target="tpu_custom_call" | custom-call | flops 1000 | bytes 1000 | tf_op jit(solution)/shard_map/other_odd/pallas_call | solution.py:277
  5.6 0.1 collective-permute-start.3
  5.7 0.0 copy-done
  5.7 1.7 %own_even.1 = (bf16[128,16,128]{2,1,0:T(8,128)(2,1)S(1)}, f32[128,128]{1,0:T(8,128)S(1)}, f32[128,128]{1,0:T(8,128)S(1)}, f32[128,128]{1,0:T(8,128)S(1)}, f32[12...) custom-call(bf16[8,2,2,128,256]{4,3,2,1,0:T(8,128)(2,1)S(1)} %get-tuple-elemen, ...), custom_call_target="tpu_custom_call" | custom-call | flops 1000 | bytes 1000 | tf_op jit(solution)/shard_map/own_even/pallas_call | solution.py:267
  7.4 0.0 collective-permute-done.moved_ref
  7.4 0.1 add_even.1
  7.5 0.1 collective-permute-start.1
  7.6 3.3 %collective-permute-start.2 = (bf16[16,16,128]{2,1,0:T(8,128)(2,1)S(1)}, bf16[16,16,128]{2,1,0:T(8,128)(2,1)S(1)}, u32[]{:S(2)}, u32[]{:S(2)}) collective-permute-start(bf16[16,16,128]{2,1,0:T(8,128)(2,1)S(1)} %get-tuple-element.42), channel_id=1, source_target_pairs={{0,10},{2,8},{4,14},{6,12},{8,2},{10,0},{12,6},{14,4},{1,11},{3,9}... | collective-permute-start | bytes 196616 | tf_op jit(solution)/shard_map/ppermute | solution.py:482
  10.9 0.0 copy-start.1
  10.9 0.9 %own_odd.1.own_ref = bf16[128,16,128]{2,1,0:T(8,128)(2,1)S(1)} custom-call(bf16[8,2,2,128,256]{4,3,2,1,0:T(8,128)(2,1)S(1)} %get-tuple-element.34.field_ref, f32[128,128]{1,0:T(8,128)S(1)} %get-tuple-element.43.refs_0_, f32[128,128]{1,0:T(8,128)S(1)} %get-tuple-element.44.refs_1_, f32[128,128]{1,0:T(8,128)S(1)} %get-tuple-element.45.refs_2_, ...), custom_call_target="tpu_custom_call" | custom-call | flops 1000 | bytes 1000 | tf_op jit(solution)/shard_map/own_odd/pallas_call | solution.py:277
  11.8 0.0 collective-permute-done.3.moved_ref
  11.8 0.1 add_odd.1
  12.0 0.1 collective-permute-start.6
  12.1 2.3 %collective-permute-start.7 = (bf16[16,16,128]{2,1,0:T(8,128)(2,1)S(1)}, bf16[16,16,128]{2,1,0:T(8,128)(2,1)S(1)}, u32[]{:S(2)}, u32[]{:S(2)}) collective-permute-start(bf16[16,16,128]{2,1,0:T(8,128)(2,1)S(1)} %get-tuple-element.61), channel_id=1, source_target_pairs={{0,10},{2,8},{4,14},{6,12},{8,2},{10,0},{12,6},{14,4},{1,11},{3,9}... | collective-permute-start | bytes 196616 | tf_op jit(solution)/shard_map/ppermute | solution.py:482
  14.4 0.2 collective-permute-start.4
  14.6 0.0 collective-permute-done.1.refs_0_
  14.6 2.2 %collective-permute-start.5 = (bf16[16,32,128]{2,1,0:T(8,128)(2,1)S(1)}, bf16[16,32,128]{2,1,0:T(8,128)(2,1)S(1)}, u32[]{:S(2)}, u32[]{:S(2)}) collective-permute-start(bf16[16,32,128]{2,1,0:T(8,128)(2,1)S(1)} %get-tuple-element.59), channel_id=1, source_target_pairs={{0,14},{2,12},{4,10},{6,8},{8,6},{10,4},{12,2},{14,0},{1,15},{3,13... | collective-permute-start | bytes 393224 | tf_op jit(solution)/shard_map/ppermute | solution.py:482
  16.8 0.0 collective-permute-done.2.refs_1_
  16.8 10.5 %collective-permute-start.8 = (bf16[16,32,128]{2,1,0:T(8,128)(2,1)S(1)}, bf16[16,32,128]{2,1,0:T(8,128)(2,1)S(1)}, u32[]{:S(2)}, u32[]{:S(2)}) collective-permute-start(bf16[16,32,128]{2,1,0:T(8,128)(2,1)S(1)} %get-tuple-element.62), channel_id=1, source_target_pairs={{0,4},{2,6},{4,0},{6,2},{8,12},{10,14},{12,8},{14,10},{1,5},{3,7},... | collective-permute-start | bytes 393224 | tf_op jit(solution)/shard_map/ppermute | solution.py:482
  27.3 0.0 collective-permute-done.6.refs_4_
  27.3 1.4 %collective-permute-start.9 = (bf16[16,32,128]{2,1,0:T(8,128)(2,1)S(1)}, bf16[16,32,128]{2,1,0:T(8,128)(2,1)S(1)}, u32[]{:S(2)}, u32[]{:S(2)}) collective-permute-start(bf16[16,32,128]{2,1,0:T(8,128)(2,1)S(1)} %get-tuple-element.63), channel_id=1, source_target_pairs={{0,6},{2,4},{4,2},{6,0},{8,14},{10,12},{12,10},{14,8},{1,7},{3,5},... | collective-permute-start | bytes 393224 | tf_op jit(solution)/shard_map/ppermute | solution.py:482
  28.7 0.0 collective-permute-done.7.refs_5_
  28.7 0.0 collective-permute-start.10
  28.7 0.3 table.1.refs_10_
  29.0 1.6 %collective-permute-done.4.refs_2_ = bf16[16,32,128]{2,1,0:T(8,128)(2,1)S(1)} collective-permute-done((bf16[16,32,128]{2,1,0:T(8,128)(2,1)S(1)}, bf16[16,32,128]{2,1,0:T(8,128)(2,1)S(1)}, u32[]{:S(2)}, u32[]{:S(2)}) %collective-permute-start.4) | collective-permute-done | bytes 131104 | tf_op jit(solution)/shard_map/ppermute | solution.py:482
  30.6 5.7 %collective-permute-done.5.refs_3_ = bf16[16,32,128]{2,1,0:T(8,128)(2,1)S(1)} collective-permute-done((bf16[16,32,128]{2,1,0:T(8,128)(2,1)S(1)}, bf16[16,32,128]{2,1,0:T(8,128)(2,1)S(1)}, u32[]{:S(2)}, u32[]{:S(2)}) %collective-permute-start.5) | collective-permute-done | bytes 131104 | tf_op jit(solution)/shard_map/ppermute | solution.py:482
  36.3 0.0 collective-permute-done.8.refs_6_
  36.3 0.0 collective-permute-done.9.refs_7_
  36.3 2.9 %collective-permute-done.10.refs_8_ = bf16[16,32,128]{2,1,0:T(8,128)(2,1)S(1)} collective-permute-done((bf16[16,32,128]{2,1,0:T(8,128)(2,1)S(1)}, bf16[16,32,128]{2,1,0:T(8,128)(2,1)S(1)}, u32[]{:S(2)}, u32[]{:S(2)}) %collective-permute-start.10) | collective-permute-done | bytes 131104 | tf_op jit(solution)/shard_map/ppermute | solution.py:482
  39.2 0.0 copy-done.1
  39.2 1.4 %peaks.1 = (f32[1,16]{1,0:T(1,128)}, f32[1,16]{1,0:T(1,128)}) custom-call(bf16[16,16,128]{2,1,0:T(8,128)(2,1)S(1)} %collective-permute-done.1.refs_0_, bf16[16,16,128]{2,1,0:T(8,128)(2,1)S(1)} %collective-permute-done.2.refs_1_, bf16[16,32,128]{2,1,0:T(8,128)(2,1)S(1)} %collective-permute-done.4.refs_2_, ...), custom_call_target="tpu_custom_call" | custom-call | tf_op jit(solution)/shard_map/peaks/pallas_call | solution.py:435
Async XLA Ops:
  3.9 1.8 %copy-start = (s32[8]{0:T(128)S(1)}, s32[8]{0:T(128)}, u32[]{:S(2)}) copy-start(s32[8]{0:T(128)} %refs_1_.1) | copy-start | bytes 100
  3.9 3.5 %collective-permute-start = (bf16[128,16,128]{2,1,0:T(8,128)(2,1)S(1)}, bf16[128,16,128]{2,1,0:T(8,128)(2,1)S(1)}, u32[]{:S(2)}, u32[]{:S(2)}) collective-permute-start(bf16[128,16,128]{2,1,0:T(8,128)(2,1)S(1)} %get-tuple-element.40), channel_id=1, source_target_pairs={{0,1},{1,0},{2,3},{3,2},{4,5},{5,4},{6,7},{7,6},{8,9},{9,8},{10,11... | collective-permute-start | bytes 1572872 | tf_op jit(solution)/shard_map/ppermute | solution.py:266
  5.6 6.2 %collective-permute-start.3 = (bf16[128,16,128]{2,1,0:T(8,128)(2,1)S(1)}, bf16[128,16,128]{2,1,0:T(8,128)(2,1)S(1)}, u32[]{:S(2)}, u32[]{:S(2)}) collective-permute-start(bf16[128,16,128]{2,1,0:T(8,128)(2,1)S(1)} %other_odd.1), channel_id=1, source_target_pairs={{0,1},{1,0},{2,3},{3,2},{4,5},{5,4},{6,7},{7,6},{8,9},{9,8},{10,11... | collective-permute-start | bytes 1572872 | tf_op jit(solution)/shard_map/ppermute | solution.py:289
  7.5 7.0 %collective-permute-start.1 = (bf16[16,16,128]{2,1,0:T(8,128)(2,1)S(1)}, bf16[16,16,128]{2,1,0:T(8,128)(2,1)S(1)}, u32[]{:S(2)}, u32[]{:S(2)}) collective-permute-start(bf16[16,16,128]{2,1,0:T(8,128)(2,1)S(1)} %get-tuple-element.41), channel_id=1, source_target_pairs={{0,8},{2,10},{4,12},{6,14},{8,0},{10,2},{12,4},{14,6},{1,9},{3,11}... | collective-permute-start | bytes 196616 | tf_op jit(solution)/shard_map/ppermute | solution.py:482
  7.6 9.1 %collective-permute-start.2 = (bf16[16,16,128]{2,1,0:T(8,128)(2,1)S(1)}, bf16[16,16,128]{2,1,0:T(8,128)(2,1)S(1)}, u32[]{:S(2)}, u32[]{:S(2)}) collective-permute-start(bf16[16,16,128]{2,1,0:T(8,128)(2,1)S(1)} %get-tuple-element.42), channel_id=1, source_target_pairs={{0,10},{2,8},{4,14},{6,12},{8,2},{10,0},{12,6},{14,4},{1,11},{3,9}... | collective-permute-start | bytes 196616 | tf_op jit(solution)/shard_map/ppermute | solution.py:482
  10.9 28.3 %copy-start.1 = (f32[1,16]{1,0:T(1,128)S(1)}, f32[1,16]{1,0:T(1,128)}, u32[]{:S(2)}) copy-start(f32[1,16]{1,0:T(1,128)} %refs_11_.1) | copy-start | bytes 196
  12.0 15.3 %collective-permute-start.6 = (bf16[16,16,128]{2,1,0:T(8,128)(2,1)S(1)}, bf16[16,16,128]{2,1,0:T(8,128)(2,1)S(1)}, u32[]{:S(2)}, u32[]{:S(2)}) collective-permute-start(bf16[16,16,128]{2,1,0:T(8,128)(2,1)S(1)} %get-tuple-element.60), channel_id=1, source_target_pairs={{0,8},{2,10},{4,12},{6,14},{8,0},{10,2},{12,4},{14,6},{1,9},{3,11}... | collective-permute-start | bytes 196616 | tf_op jit(solution)/shard_map/ppermute | solution.py:482
  12.1 16.6 %collective-permute-start.7 = (bf16[16,16,128]{2,1,0:T(8,128)(2,1)S(1)}, bf16[16,16,128]{2,1,0:T(8,128)(2,1)S(1)}, u32[]{:S(2)}, u32[]{:S(2)}) collective-permute-start(bf16[16,16,128]{2,1,0:T(8,128)(2,1)S(1)} %get-tuple-element.61), channel_id=1, source_target_pairs={{0,10},{2,8},{4,14},{6,12},{8,2},{10,0},{12,6},{14,4},{1,11},{3,9}... | collective-permute-start | bytes 196616 | tf_op jit(solution)/shard_map/ppermute | solution.py:482
  14.4 16.3 %collective-permute-start.4 = (bf16[16,32,128]{2,1,0:T(8,128)(2,1)S(1)}, bf16[16,32,128]{2,1,0:T(8,128)(2,1)S(1)}, u32[]{:S(2)}, u32[]{:S(2)}) collective-permute-start(bf16[16,32,128]{2,1,0:T(8,128)(2,1)S(1)} %get-tuple-element.58), channel_id=1, source_target_pairs={{0,12},{2,14},{4,8},{6,10},{8,4},{10,6},{12,0},{14,2},{1,13},{3,15... | collective-permute-start | bytes 393224 | tf_op jit(solution)/shard_map/ppermute | solution.py:482
  14.6 21.8 %collective-permute-start.5 = (bf16[16,32,128]{2,1,0:T(8,128)(2,1)S(1)}, bf16[16,32,128]{2,1,0:T(8,128)(2,1)S(1)}, u32[]{:S(2)}, u32[]{:S(2)}) collective-permute-start(bf16[16,32,128]{2,1,0:T(8,128)(2,1)S(1)} %get-tuple-element.59), channel_id=1, source_target_pairs={{0,14},{2,12},{4,10},{6,8},{8,6},{10,4},{12,2},{14,0},{1,15},{3,13... | collective-permute-start | bytes 393224 | tf_op jit(solution)/shard_map/ppermute | solution.py:482
  16.8 19.6 %collective-permute-start.8 = (bf16[16,32,128]{2,1,0:T(8,128)(2,1)S(1)}, bf16[16,32,128]{2,1,0:T(8,128)(2,1)S(1)}, u32[]{:S(2)}, u32[]{:S(2)}) collective-permute-start(bf16[16,32,128]{2,1,0:T(8,128)(2,1)S(1)} %get-tuple-element.62), channel_id=1, source_target_pairs={{0,4},{2,6},{4,0},{6,2},{8,12},{10,14},{12,8},{14,10},{1,5},{3,7},... | collective-permute-start | bytes 393224 | tf_op jit(solution)/shard_map/ppermute | solution.py:482
  27.3 9.1 %collective-permute-start.9 = (bf16[16,32,128]{2,1,0:T(8,128)(2,1)S(1)}, bf16[16,32,128]{2,1,0:T(8,128)(2,1)S(1)}, u32[]{:S(2)}, u32[]{:S(2)}) collective-permute-start(bf16[16,32,128]{2,1,0:T(8,128)(2,1)S(1)} %get-tuple-element.63), channel_id=1, source_target_pairs={{0,6},{2,4},{4,2},{6,0},{8,14},{10,12},{12,10},{14,8},{1,7},{3,5},... | collective-permute-start | bytes 393224 | tf_op jit(solution)/shard_map/ppermute | solution.py:482
  28.7 10.5 %collective-permute-start.10 = (bf16[16,32,128]{2,1,0:T(8,128)(2,1)S(1)}, bf16[16,32,128]{2,1,0:T(8,128)(2,1)S(1)}, u32[]{:S(2)}, u32[]{:S(2)}) collective-permute-start(bf16[16,32,128]{2,1,0:T(8,128)(2,1)S(1)} %get-tuple-element.64), channel_id=1, source_target_pairs={{0,2},{2,0},{4,6},{6,4},{8,10},{10,8},{12,14},{14,12},{1,3},{3,1},... | collective-permute-start | bytes 393224 | tf_op jit(solution)/shard_map/ppermute | solution.py:482
where the time goes:
time: 40.7 us; the launch traced here: 40.6 us
  starting transfers between devices  20.9 us (51%)
  waiting for transfers between devices  10.2 us (25%)
  Pallas kernels  8.73 us (21%)
  between operations  0.73 us (2%)
    ppermute x9, starting transfers between devices, send(): return lax.ppermute(array, 'freq', pairs)  20.1 us
    ppermute x9, waiting for transfers between devices, send(): return lax.ppermute(array, 'freq', pairs)  10.2 us
    pallas_call x1, Pallas kernels, even_partials(): call(functools.partial(other_even_kernel, freq_total, slots), 'other_even...  3.24 us
    pallas_call x2, Pallas kernels, odd_partials(): call(functools.partial(odd_kernel, len(first)), name, [vmem] * 8 + [pl.Bl...  1.86 us
    pallas_call x1, Pallas kernels, even_partials(): call(functools.partial(own_even_kernel, freq_total, slots), 'own_even', [...  1.71 us
    pallas_call x1, Pallas kernels, peaks(): pl.pallas_call(functools.partial(peak_kernel, freq_total, folded, sources...  1.37 us
  transfers between devices with their start and end apart: 11, of which 3 were waited for; matrix products, arithmetic and copies ran while one was open for 0% of the time, Pallas kernels for 10%

commit v1 on v0

v1 whole, which is shorter than its diff:
```python
import functools
import math

import jax
import jax.numpy as jnp
from jax import lax
from jax.experimental import pallas as pl
from jax.experimental.pallas import tpu as pltpu
from jax.sharding import PartitionSpec as P

W_DEV = 16
W_HALF = W_DEV // 2
FG = 128
NB = 4
SB = 32
T_CAP = 1024

EDGE = 0.6
STEEP = 3.0
EPS = 1e-05

ROWS = NB * SB
VMEM_BYTES = 48 * 1024 * 1024


def sin_half_turn(turns):
    angle = turns * math.pi
    square = angle * angle
    sine = 1.0 / 6227020800.0
    for factorial in (-39916800.0, 362880.0, -5040.0, 120.0, -6.0, 1.0):
        sine = sine * square + 1.0 / factorial
    cosine = 1.0 / 479001600.0
    for factorial in (-3628800.0, 40320.0, -720.0, 24.0, -2.0, 1.0):
        cosine = cosine * square + 1.0 / factorial
    return sine * angle, cosine


def sincos_turns(turns):
    rest = turns - jnp.floor(turns + 0.5)
    sine, cosine = sin_half_turn(rest)
    return 2.0 * sine * cosine, 1.0 - 2.0 * sine * sine


def dot(left, right, contract):
    return lax.dot_general(
        left, right, (contract, ((), ())), preferred_element_type=jnp.float32
    )


def slot_masks(slots):
    half = slots // 2
    between = (2, half, half + 1, 3, slots - 1)
    return (0, 1, *between, slots - 2), (0, slots - 2, *between, 1)


def partner(slots, slot):
    index = lax.axis_index("freq")
    inner = ((index * 2) ^ index) & (slots // 2) != 0
    outer_masks, inner_masks = slot_masks(slots)
    mask = jnp.zeros_like(slot)
    for s in range(1, slots):
        mask = jnp.where(slot == s, jnp.where(inner, inner_masks[s], outer_masks[s]), mask)
    return mask ^ index


def slot_order(slots):
    size = FG // slots
    row = lax.broadcasted_iota(jnp.int32, (FG, 1), 0)
    column = lax.broadcasted_iota(jnp.int32, (FG, FG), 1)
    if slots > 1:
        row = partner(slots, row // size) * size + row % size
    return row == column


def flaw_pick(slots, which, cells_ref):
    cells = jnp.where(which == 0, cells_ref[:, :FG], cells_ref[:, FG:])
    cell_sel = lax.broadcasted_iota(jnp.int32, (cells_ref.shape[1], FG), 0) == cells
    return dot(
        slot_order(slots).astype(jnp.bfloat16), cell_sel.astype(jnp.bfloat16), ((1,), (1,))
    ).astype(jnp.bfloat16)


def delay_pieces(channel_ref, delay_ref, elements):
    channel_sel = (
        (
            lax.broadcasted_iota(jnp.int32, (delay_ref.shape[0], elements), 0)
            == channel_ref[...]
        )
        .astype(jnp.float32)
        .T.astype(jnp.bfloat16)
    )
    rest = delay_ref[...]
    pieces = []
    for _ in range(3):
        piece = rest.astype(jnp.bfloat16)
        rest = rest - piece.astype(jnp.float32)
        pieces.append(dot(channel_sel, piece, ((1,), (0,))).astype(jnp.bfloat16))
    return pieces


def turned(law, step):
    return law[0] * step[0] - law[1] * step[1], law[1] * step[0] + law[0] * step[1]


def prepare(freq_total, slots, which, pieces, size_ref, slope_ref, blocks_ref):
    first_freq = lax.axis_index("freq") * W_DEV
    order = slot_order(slots)
    size = size_ref[pl.ds(which, 1), :]
    turn = size * slope_ref[pl.ds(which, 1), :] * (1.0 / freq_total)
    size = jnp.sum(jnp.where(order, size, 0.0), axis=1, keepdims=True)
    turn = jnp.sum(jnp.where(order, turn, 0.0), axis=1, keepdims=True)
    freq = first_freq + lax.broadcasted_iota(jnp.int32, (FG, FG), 1)
    sine, cosine = sincos_turns(turn * freq.astype(jnp.float32))
    k_real = size * (1.0 + EDGE) * cosine
    k_imag = size * (EDGE - 1.0) * sine
    lane = lax.broadcasted_iota(jnp.int32, (1, ROWS), 1)
    position = lane & (SB - 1)
    for j in range(NB):
        block = blocks_ref[which * NB + j]
        position = position + jnp.where((lane >> 5) == j, block * SB, 0)
    scan_sel = (
        lax.broadcasted_iota(jnp.int32, (pieces[0].shape[1], ROWS), 0) == position
    ).astype(jnp.bfloat16)
    delays = None
    for piece in pieces:
        moved = dot(piece, scan_sel, ((1,), (0,)))
        delays = moved if delays is None else delays + moved
    phase = delays * (0.5 / freq_total)
    unit = sincos_turns(phase)[::-1]
    base = sincos_turns(phase * first_freq.astype(jnp.float32))[::-1]
    return base, turned(unit, unit), turned(base, unit), k_real, k_imag


def store_law(law_ref, law, step):
    elements = law_ref.shape[1] // 2
    for w in range(W_HALF):
        c = law[0].astype(jnp.bfloat16)
        s = law[1].astype(jnp.bfloat16)
        law_ref[w, :elements, :ROWS] = c
        law_ref[w, :elements, ROWS:] = -s
        law_ref[w, elements:, :ROWS] = s
        law_ref[w, elements:, ROWS:] = c
        if w < W_HALF - 1:
            law = turned(law, step)


def pick_fields(parity, picks, field_ref, wait, picked_refs):
    elements, sites = field_ref.shape[3:]
    for w in range(W_HALF):
        wait(w)
        picked = dot(
            picks, field_ref[w, parity].reshape(2 * elements, sites), ((1,), (1,))
        ).astype(jnp.bfloat16)
        for i, ref in enumerate(picked_refs):
            ref[w] = picked[i * FG : (i + 1) * FG]


def store_spectra(parity, picked_ref, law_ref, k_real, k_imag, rows_ref, first, planes):
    for w in range(W_HALF):
        product = dot(picked_ref[w], law_ref[w], ((1,), (0,)))
        real_part = product[:, :ROWS]
        imag_part = product[:, ROWS:]
        kr = k_real[:, 2 * w + parity : 2 * w + parity + 1]
        ki = k_imag[:, 2 * w + parity : 2 * w + parity + 1]
        rows_ref[pl.ds(first + 2 * w, FG, stride=planes), :] = (
            kr * real_part - ki * imag_part
        )
        rows_ref[pl.ds(first + 2 * w + 1, FG, stride=planes), :] = (
            kr * imag_part + ki * real_part
        )


def other_even_kernel(freq_total, slots, *refs):
    field_hbm, *small_hbm = refs[:7]
    out_ref, own_picked_ref, field_ref, size_ref, slope_ref, pieces_ref, *kept = refs[7:20]
    cells_ref, channel_ref, delay_ref, blocks_ref, field_sem, small_sem, *scratch = refs[20:]
    picked_ref, law_ref, rows_ref = scratch
    small = (cells_ref, size_ref, slope_ref, channel_ref, delay_ref, blocks_ref)
    copies = [
        pltpu.make_async_copy(source, target, small_sem.at[i])
        for i, (source, target) in enumerate(zip(small_hbm, small))
    ]
    for copy in copies:
        copy.start()
    part = W_HALF // 2
    field_copies = [
        pltpu.make_async_copy(
            field_hbm.at[pl.ds(i * part, part), parity],
            field_ref.at[pl.ds(i * part, part), parity],
            field_sem.at[parity, i],
        )
        for parity in range(2)
        for i in range(2)
    ]
    for copy in field_copies:
        copy.start()
    for copy in copies:
        copy.wait()
    group = lax.axis_index("elem")
    other = 1 - group
    pieces = delay_pieces(channel_ref, delay_ref, field_ref.shape[3])
    for i, piece in enumerate(pieces):
        pieces_ref[i] = piece
    picks = jnp.concatenate(
        [flaw_pick(slots, which, cells_ref) for which in (other, group)], axis=0
    )
    even, step, odd, k_real, k_imag = prepare(
        freq_total, slots, other, pieces, size_ref, slope_ref, blocks_ref
    )
    for ref, value in zip(kept, (*step, *odd, picks, k_real, k_imag)):
        ref[...] = value
    store_law(law_ref, even, step)

    def wait(w):
        if w % part == 0:
            field_copies[w // part].wait()

    pick_fields(0, picks, field_ref, wait, (picked_ref, own_picked_ref))
    store_spectra(0, picked_ref, law_ref, k_real, k_imag, rows_ref, 0, W_DEV)
    out_ref[...] = rows_ref[...].reshape(out_ref.shape).astype(jnp.bfloat16)
    for copy in field_copies[2:]:
        copy.wait()


def other_odd_kernel(field_ref, *refs):
    step, odd, (picks_ref, k_real_ref, k_imag_ref) = refs[:2], refs[2:4], refs[4:7]
    out_ref, own_picked_ref, picked_ref, law_ref, rows_ref = refs[7:]
    store_law(law_ref, [ref[...] for ref in odd], [ref[...] for ref in step])
    pick_fields(
        1, picks_ref[...], field_ref, lambda w: None, (picked_ref, own_picked_ref)
    )
    store_spectra(1, picked_ref, law_ref, k_real_ref, k_imag_ref, rows_ref, 0, W_DEV)
    out_ref[...] = rows_ref[...].reshape(out_ref.shape).astype(jnp.bfloat16)


def own_kernel(freq_total, slots, *refs):
    *picked_refs, size_ref, slope_ref, pieces_ref, blocks_ref = refs[:6]
    out_ref, law_ref, rows_ref = refs[6:]
    pieces = [pieces_ref[i] for i in range(pieces_ref.shape[0])]
    group = lax.axis_index("elem")
    even, step, odd, k_real, k_imag = prepare(
        freq_total, slots, group, pieces, size_ref, slope_ref, blocks_ref
    )
    for parity, law in enumerate((even, odd)):
        store_law(law_ref.at[parity], law, step)
    for parity in range(2):
        store_spectra(
            parity,
            picked_refs[parity],
            law_ref.at[parity],
            k_real,
            k_imag,
            rows_ref,
            parity * W_DEV,
            2 * W_DEV,
        )
    out_ref[...] = rows_ref[...].reshape(out_ref.shape).astype(jnp.bfloat16)


def call(kernel, name, in_specs, out_shape, scratch):
    vmem = pl.BlockSpec(memory_space=pltpu.VMEM)
    return pl.pallas_call(
        kernel,
        in_specs=in_specs,
        out_specs=[vmem] * len(out_shape),
        out_shape=out_shape,
        scratch_shapes=scratch,
        compiler_params=pltpu.CompilerParams(vmem_limit_bytes=VMEM_BYTES),
        cost_estimate=pl.CostEstimate(flops=1000, bytes_accessed=1000, transcendentals=0),
        name=name,
    )


def partials(field, small, swap, freq_total, slots):
    elements, sites = field.shape[3:]
    vmem = pl.BlockSpec(memory_space=pltpu.VMEM)
    hbm = pl.BlockSpec(memory_space=pltpu.HBM)
    smem = pl.BlockSpec(memory_space=pltpu.SMEM)
    cells, size, slope, channel, delay, blocks = small
    pinned = [pltpu.with_memory_space_constraint(a, pltpu.HBM) for a in (field, *small)]
    out = jax.ShapeDtypeStruct((FG, W_DEV, ROWS), jnp.bfloat16)
    picked = jax.ShapeDtypeStruct((W_HALF, FG, 2 * elements), jnp.bfloat16)
    pieces = jax.ShapeDtypeStruct((3, elements, delay.shape[1]), jnp.bfloat16)
    kept = [jax.ShapeDtypeStruct((elements, ROWS), jnp.float32)] * 4
    kept += [jax.ShapeDtypeStruct((2 * FG, sites), jnp.bfloat16)]
    kept += [jax.ShapeDtypeStruct((FG, FG), jnp.float32)] * 2
    copied = [jax.ShapeDtypeStruct(a.shape, a.dtype) for a in (field, size, slope)]
    law = (W_HALF, 2 * elements, 2 * ROWS)
    work = [
        pltpu.VMEM(picked.shape, picked.dtype),
        pltpu.VMEM(law, jnp.bfloat16),
        pltpu.VMEM((FG * W_DEV, ROWS), jnp.float32),
    ]
    even, even_picked, field, size, slope, pieces, *kept = call(
        functools.partial(other_even_kernel, freq_total, slots),
        "other_even",
        [hbm] * len(pinned),
        [out, picked, *copied, pieces, *kept],
        [
            pltpu.VMEM(cells.shape, cells.dtype),
            pltpu.VMEM(channel.shape, channel.dtype),
            pltpu.VMEM(delay.shape, delay.dtype),
            pltpu.SMEM(blocks.shape, blocks.dtype),
            pltpu.SemaphoreType.DMA((2, 2)),
            pltpu.SemaphoreType.DMA((len(small),)),
            *work,
        ],
    )(*pinned)
    even = lax.ppermute(even, "elem", swap)
    odd, odd_picked = call(
        other_odd_kernel, "other_odd", [vmem] * 8, [out, picked], work
    )(field, *kept)
    odd = lax.ppermute(odd, "elem", swap)
    (own,) = call(
        functools.partial(own_kernel, freq_total, slots),
        "own",
        [vmem] * 5 + [smem],
        [jax.ShapeDtypeStruct((FG, 2 * W_DEV, ROWS), jnp.bfloat16)],
        [
            pltpu.VMEM((2, *law), jnp.bfloat16),
            pltpu.VMEM((FG * 2 * W_DEV, ROWS), jnp.float32),
        ],
    )(even_picked, odd_picked, size, slope, pieces, blocks)
    return own, even, odd


def add_kernel(own_ref, even_ref, odd_ref, *refs):
    size = refs[0].shape[0]
    for slot, ref in enumerate(refs):
        rows = pl.ds(slot * size, size)
        for parity, moved_ref in enumerate((even_ref, odd_ref)):
            planes = slice(parity * W_DEV, (parity + 1) * W_DEV)
            ref[:, planes] = (
                own_ref[rows, planes].astype(jnp.float32)
                + moved_ref[rows].astype(jnp.float32)
            ).astype(jnp.bfloat16)


def add(own, even, odd, slots):
    vmem = pl.BlockSpec(memory_space=pltpu.VMEM)
    shape = jax.ShapeDtypeStruct((FG // slots, *own.shape[1:]), own.dtype)
    return call(add_kernel, "add", [vmem] * 3, [shape] * slots, [])(own, even, odd)


def table_kernel(freq_total, slots, table_ref):
    height, depth = table_ref.shape[2:]
    time_block = height // 2
    row = lax.broadcasted_iota(jnp.int32, (height, depth // 2), 0)
    column = lax.broadcasted_iota(jnp.int32, (height, depth // 2), 1)
    out_imag = (row >= time_block).astype(jnp.int32)
    time = pl.program_id(0) * time_block + row - out_imag * time_block
    for parity in range(2):
        freq = (column >> 1) * 2 + parity
        if slots > 1:
            lane = lax.broadcasted_iota(jnp.int32, (1, depth // 2), 1)
            lane = (lane >> 1) * 2 + parity
            freq = partner(slots, lane // W_DEV) * W_DEV + lane % W_DEV
        steps = freq * time + ((column & 1) - out_imag) * (freq_total // 2)
        steps = (steps + 2 * freq_total) & (2 * freq_total - 1)
        _, value = sincos_turns(steps.astype(jnp.float32) * (0.5 / freq_total))
        high = value.astype(jnp.bfloat16)
        table_ref[0, parity, :, : depth // 2] = high
        table_ref[0, parity, :, depth // 2 :] = (
            value - high.astype(jnp.float32)
        ).astype(jnp.bfloat16)


def table(freq_total, slots, times, time_block):
    blocks = times // time_block
    shape = (blocks, 2, 2 * time_block, 2 * freq_total)
    return pl.pallas_call(
        functools.partial(table_kernel, freq_total, slots),
        grid=(blocks,),
        out_specs=pl.BlockSpec((1, *shape[1:]), lambda i: (i, 0, 0, 0)),
        out_shape=jax.ShapeDtypeStruct(shape, jnp.bfloat16),
        compiler_params=pltpu.CompilerParams(vmem_limit_bytes=VMEM_BYTES),
        name="table",
    )()


def peak_kernel(freq_total, folded, sources, *refs):
    count = len(refs) - 5
    table_ref, noise_ref, peak_ref, found_ref, best_ref = refs[count:]
    step = pl.program_id(0)
    columns = peak_ref.shape[1]
    time_block = table_ref.shape[2] // 2

    @pl.when(step == 0)
    def _():
        best_ref[...] = jnp.zeros_like(best_ref)

    width = min(2, columns)
    for first in range(0, columns, width):
        parts = []
        for parity in range(2):
            planes = slice(parity * W_DEV, (parity + 1) * W_DEV)
            spectra = jnp.concatenate(
                [
                    jnp.concatenate(
                        [
                            refs[i][row + first + k, planes, :]
                            for i, row in sources
                        ]
                        * 2,
                        axis=0,
                    )
                    for k in range(width)
                ],
                axis=1,
            )
            parts.append(dot(table_ref[0, parity], spectra, ((1,), (0,))))
        powers = []
        for signal in [parts[0] + parts[1]] + [parts[0] - parts[1]] * folded:
            real_part = signal[:time_block]
            imag_part = signal[time_block:]
            powers.append(real_part * real_part + imag_part * imag_part)
        power = jnp.maximum(powers[0], powers[-1]) if folded else powers[0]
        power = jnp.max(power, axis=0, keepdims=True)
        for k in range(width):
            row = pl.ds(first + k, 1)
            best_ref[row, :] = jnp.maximum(
                best_ref[row, :], power[:, k * ROWS : (k + 1) * ROWS]
            )

    @pl.when(step == pl.num_programs(0) - 1)
    def _():
        largest = jnp.max(best_ref[...], axis=1, keepdims=True)
        shape = best_ref.shape
        diagonal = lax.broadcasted_iota(jnp.int32, shape, 0) == lax.broadcasted_iota(
            jnp.int32, shape, 1
        )
        largest = jnp.max(jnp.where(diagonal, largest, 0.0), axis=0, keepdims=True)
        peak = jnp.sqrt(largest[:, :columns]) * (1.0 / math.sqrt(freq_total))
        score = STEEP * (jnp.log(peak + EPS) - jnp.log(noise_ref[...]))
        peak_ref[...] = peak
        found_ref[...] = 1.0 / (1.0 + jnp.exp(-score))


def peaks(spectra, sources, twiddles, noise_level, freq_total, folded):
    columns = noise_level.shape[1]
    out_spec = pl.BlockSpec((1, columns), lambda i: (0, 0))
    return pl.pallas_call(
        functools.partial(peak_kernel, freq_total, folded, sources),
        grid=(twiddles.shape[0],),
        in_specs=[pl.BlockSpec(a.shape, lambda i: (0, 0, 0)) for a in spectra]
        + [pl.BlockSpec((1, *twiddles.shape[1:]), lambda i: (i, 0, 0, 0)), out_spec],
        out_specs=[out_spec, out_spec],
        out_shape=[jax.ShapeDtypeStruct((1, columns), jnp.float32)] * 2,
        scratch_shapes=[pltpu.VMEM((max(8, columns), ROWS), jnp.float32)],
        compiler_params=pltpu.CompilerParams(vmem_limit_bytes=VMEM_BYTES),
        name="peaks",
    )(*spectra, twiddles, noise_level)


def body(
    flaw_cells,
    flaw_blocks,
    element_channel,
    focal_delay,
    beam_field,
    flaw_size,
    flaw_slope,
    noise_level,
):
    freq_count = lax.axis_size("freq")
    freq_total = W_DEV * freq_count
    sample_count = min(T_CAP, 2 * freq_total)
    swap = [(0, 1), (1, 0)]
    direct = freq_count == 8
    slots = freq_count if direct else 1
    small = (
        flaw_cells.reshape(1, -1),
        flaw_size,
        flaw_slope,
        element_channel.reshape(1, -1),
        focal_delay,
        flaw_blocks,
    )
    folded = sample_count == 2 * freq_total
    times = sample_count // 2 if folded else sample_count
    twiddles = table(freq_total, slots, times, min(128, times))
    field = beam_field.reshape(W_HALF, 2, *beam_field.shape[1:])
    parts = add(*partials(field, small, swap, freq_total, slots), slots)
    if direct:
        half = slots // 2
        spectra = []
        for slot, masks in enumerate(zip(*slot_masks(slots))):
            pairs = [(a, a ^ masks[((2 * a) ^ a) & half != 0]) for a in range(slots)]
            spectra.append(lax.ppermute(parts[slot], "freq", pairs) if slot else parts[slot])
        spectra = [*spectra[1:], spectra[0]]
        sources = [((slot - 1) % slots, 0) for slot in range(slots)]
    else:
        spectra = [
            lax.all_to_all(parts[0], "freq", split_axis=0, concat_axis=0, tiled=True)
        ]
        sources = [(0, s * (FG // freq_count)) for s in range(freq_count)]
    return tuple(peaks(spectra, sources, twiddles, noise_level, freq_total, folded))


def solution(mesh):
    in_specs = (
        P("batch"),
        P("batch"),
        P("elem"),
        P(),
        P("freq", None, "elem", None),
        P("batch", None),
        P("batch", None),
        P(("batch", "elem"), "freq"),
    )
    out_specs = (P(("batch", "elem"), "freq"), P(("batch", "elem"), "freq"))
    return jax.shard_map(body, mesh=mesh, in_specs=in_specs, out_specs=out_specs, check_vma=False)
```

time: 40.7 us -> 36.8 us (0.904)
  the two profiles are of different devices: /device:TPU:17 before, /device:TPU:0 now
where the time goes in v1:
time: 36.8 us; the launch traced here: 36.7 us
  starting transfers between devices  14.3 us (39%)
  waiting for transfers between devices  12.3 us (33%)
  Pallas kernels  9.29 us (25%)
  between operations  0.7 us (2%)
    ppermute x7, starting transfers between devices, body(): lax.ppermute(parts[slot], 'freq', pairs)  13.7 us
    ppermute x7, waiting for transfers between devices, body(): lax.ppermute(parts[slot], 'freq', pairs)  12.3 us
    pallas_call x1, Pallas kernels, partials(): call(functools.partial(other_even_kernel, freq_total, slots), 'other_even...  3.28 us
    pallas_call x1, Pallas kernels, partials(): call(functools.partial(own_kernel, freq_total, slots), 'own', [vmem] * 5...  3.1 us
    pallas_call x1, Pallas kernels, peaks(): pl.pallas_call(functools.partial(peak_kernel, freq_total, folded, sources...  1.38 us
    pallas_call x1, Pallas kernels, partials(): call(other_odd_kernel, 'other_odd', [vmem] * 8, [out, picked], work)  0.96 us
  transfers between devices with their start and end apart: 9, of which 2 were waited for; matrix products, arithmetic and copies ran while one was open for 0% of the time, Pallas kernels for 9%

profile of v1, /device:TPU:0, one launch (start us, length us, event | category | flops | bytes accessed | tf_op | source)
XLA Modules:
  0.0 36.7 jit_solution(5664894829713644367)
XLA Ops:
  0.6 0.0 copy-start
  0.6 3.3 %other_even.1 = (bf16[128,16,128]{2,1,0:T(8,128)(2,1)S(1)}, bf16[8,128,256]{2,1,0:T(8,128)(2,1)S(1)}, bf16[8,2,2,128,256]{4,3,2,1,0:T(8,128)(2,1)S(1)}, f32[2,12...) custom-call(bf16[8,2,2,128,256]{4,3,2,1,0:T(8,128)(2,1)} %bitcast.3,, ...), custom_call_target="tpu_custom_call" | custom-call | flops 1000 | bytes 1000 | tf_op jit(solution)/shard_map/other_even/pallas_call | solution.py:294
  3.9 1.0 %other_odd.1 = (bf16[128,16,128]{2,1,0:T(8,128)(2,1)S(1)}, bf16[8,128,256]{2,1,0:T(8,128)(2,1)S(1)}) custom-call(bf16[8,2,2,128,256]{4,3,2,1,0:T(8,128)(2,1)S(1)} %get-tuple-element.26.field_ref, f32[128,128]{1,0:T(8,128)S(1)} %get-tuple-element.27.refs_0_, f32[128,128]{1,0:T(8,128)S(1)} %get-tuple-element.28.refs_1_, ...), custom_call_target="tpu_custom_call" | custom-call | flops 1000 | bytes 1000 | tf_op jit(solution)/shard_map/other_odd/pallas_call | solution.py:310
  4.9 0.5 %collective-permute-start.1 = (bf16[128,16,128]{2,1,0:T(8,128)(2,1)S(1)}, bf16[128,16,128]{2,1,0:T(8,128)(2,1)S(1)}, u32[]{:S(2)}, u32[]{:S(2)}) collective-permute-start(bf16[128,16,128]{2,1,0:T(8,128)(2,1)S(1)} %get-tuple-element.39), channel_id=1, source_target_pairs={{0,1},{1,0},{2,3},{3,2},{4,5},{5,4},{6,7},{7,6},{8,9},{9,8},{10,11... | collective-permute-start | bytes 1572872 | tf_op jit(solution)/shard_map/ppermute | solution.py:313
  5.4 0.1 collective-permute-start
  5.5 0.0 copy-done
  5.5 0.0 copy-start.1
  5.5 3.1 %own.1.own_ref = bf16[128,32,128]{2,1,0:T(8,128)(2,1)S(1)} custom-call(bf16[8,128,256]{2,1,0:T(8,128)(2,1)S(1)} %get-tuple-element.25.refs_0_, bf16[8,128,256]{2,1,0:T(8,128)(2,1)S(1)} %get-tuple-element.34.refs_1_, f32[2,128]{1,0:T(2,128)S(1)} %get-tuple-element.35.refs_2_, f32[2,128]{1,0:T(2,128)S(1)} %get-tuple-element.36.refs_3_, ...), custom_call_target="tpu_custom_call" | custom-call | flops 1000 | bytes 1000 | tf_op jit(solution)/shard_map/own/pallas_call | solution.py:314
  8.6 0.0 collective-permute-done.1.odd_ref
  8.6 0.0 collective-permute-done.even_ref
  8.6 0.3 add.1
  8.9 3.0 %collective-permute-start.2 = (bf16[16,32,128]{2,1,0:T(8,128)(2,1)S(1)}, bf16[16,32,128]{2,1,0:T(8,128)(2,1)S(1)}, u32[]{:S(2)}, u32[]{:S(2)}) collective-permute-start(bf16[16,32,128]{2,1,0:T(8,128)(2,1)S(1)} %get-tuple-element.40), channel_id=1, source_target_pairs={{0,2},{2,0},{4,8},{6,10},{8,4},{10,6},{12,14},{14,12},{1,3},{3,1},... | collective-permute-start | bytes 393224 | tf_op jit(solution)/shard_map/ppermute | solution.py:489
  11.9 1.7 %collective-permute-start.3 = (bf16[16,32,128]{2,1,0:T(8,128)(2,1)S(1)}, bf16[16,32,128]{2,1,0:T(8,128)(2,1)S(1)}, u32[]{:S(2)}, u32[]{:S(2)}) collective-permute-start(bf16[16,32,128]{2,1,0:T(8,128)(2,1)S(1)} %get-tuple-element.41), channel_id=1, source_target_pairs={{0,4},{2,6},{4,0},{6,2},{8,12},{10,14},{12,8},{14,10},{1,5},{3,7},... | collective-permute-start | bytes 393224 | tf_op jit(solution)/shard_map/ppermute | solution.py:489
  13.6 2.5 %collective-permute-start.4 = (bf16[16,32,128]{2,1,0:T(8,128)(2,1)S(1)}, bf16[16,32,128]{2,1,0:T(8,128)(2,1)S(1)}, u32[]{:S(2)}, u32[]{:S(2)}) collective-permute-start(bf16[16,32,128]{2,1,0:T(8,128)(2,1)S(1)} %get-tuple-element.42), channel_id=1, source_target_pairs={{0,8},{2,10},{4,12},{6,14},{8,0},{10,2},{12,4},{14,6},{1,9},{3,11}... | collective-permute-start | bytes 393224 | tf_op jit(solution)/shard_map/ppermute | solution.py:489
  16.1 1.3 %collective-permute-start.5 = (bf16[16,32,128]{2,1,0:T(8,128)(2,1)S(1)}, bf16[16,32,128]{2,1,0:T(8,128)(2,1)S(1)}, u32[]{:S(2)}, u32[]{:S(2)}) collective-permute-start(bf16[16,32,128]{2,1,0:T(8,128)(2,1)S(1)} %get-tuple-element.43), channel_id=1, source_target_pairs={{0,10},{2,8},{4,14},{6,12},{8,2},{10,0},{12,6},{14,4},{1,11},{3,9}... | collective-permute-start | bytes 393224 | tf_op jit(solution)/shard_map/ppermute | solution.py:489
  17.4 0.3 collective-permute-start.6
  17.7 0.0 collective-permute-done.2.refs_0_
  17.7 3.6 %collective-permute-start.7 = (bf16[16,32,128]{2,1,0:T(8,128)(2,1)S(1)}, bf16[16,32,128]{2,1,0:T(8,128)(2,1)S(1)}, u32[]{:S(2)}, u32[]{:S(2)}) collective-permute-start(bf16[16,32,128]{2,1,0:T(8,128)(2,1)S(1)} %get-tuple-element.45), channel_id=1, source_target_pairs={{0,14},{2,12},{4,10},{6,8},{8,6},{10,4},{12,2},{14,0},{1,15},{3,13... | collective-permute-start | bytes 393224 | tf_op jit(solution)/shard_map/ppermute | solution.py:489
  21.3 0.0 collective-permute-done.3.refs_1_
  21.3 1.4 %collective-permute-start.8 = (bf16[16,32,128]{2,1,0:T(8,128)(2,1)S(1)}, bf16[16,32,128]{2,1,0:T(8,128)(2,1)S(1)}, u32[]{:S(2)}, u32[]{:S(2)}) collective-permute-start(bf16[16,32,128]{2,1,0:T(8,128)(2,1)S(1)} %get-tuple-element.46), channel_id=1, source_target_pairs={{0,12},{2,14},{4,6},{6,4},{8,10},{10,8},{12,0},{14,2},{1,13},{3,15... | collective-permute-start | bytes 393224 | tf_op jit(solution)/shard_map/ppermute | solution.py:489
  22.6 0.3 table.1.refs_8_
  23.0 3.5 %collective-permute-done.4.refs_2_ = bf16[16,32,128]{2,1,0:T(8,128)(2,1)S(1)} collective-permute-done((bf16[16,32,128]{2,1,0:T(8,128)(2,1)S(1)}, bf16[16,32,128]{2,1,0:T(8,128)(2,1)S(1)}, u32[]{:S(2)}, u32[]{:S(2)}) %collective-permute-start.4) | collective-permute-done | bytes 131104 | tf_op jit(solution)/shard_map/ppermute | solution.py:489
  26.5 8.8 %collective-permute-done.5.refs_3_ = bf16[16,32,128]{2,1,0:T(8,128)(2,1)S(1)} collective-permute-done((bf16[16,32,128]{2,1,0:T(8,128)(2,1)S(1)}, bf16[16,32,128]{2,1,0:T(8,128)(2,1)S(1)}, u32[]{:S(2)}, u32[]{:S(2)}) %collective-permute-start.5) | collective-permute-done | bytes 131104 | tf_op jit(solution)/shard_map/ppermute | solution.py:489
  35.3 0.0 collective-permute-done.6.refs_4_
  35.3 0.0 collective-permute-done.7.refs_5_
  35.3 0.0 collective-permute-done.8.refs_6_
  35.3 0.0 copy-done.1
  35.3 1.4 %peaks.1 = (f32[1,16]{1,0:T(1,128)}, f32[1,16]{1,0:T(1,128)}) custom-call(bf16[16,32,128]{2,1,0:T(8,128)(2,1)S(1)} %collective-permute-done.2.refs_0_, bf16[16,32,128]{2,1,0:T(8,128)(2,1)S(1)} %collective-permute-done.3.refs_1_, bf16[16,32,128]{2,1,0:T(8,128)(2,1)S(1)} %collective-permute-done.4.refs_2_, ...), custom_call_target="tpu_custom_call" | custom-call | tf_op jit(solution)/shard_map/peaks/pallas_call | solution.py:442
Async XLA Ops:
  0.6 4.9 %copy-start = (s32[8]{0:T(128)S(1)}, s32[8]{0:T(128)}, u32[]{:S(2)}) copy-start(s32[8]{0:T(128)} %refs_5_.3) | copy-start | bytes 100
  4.9 3.7 %collective-permute-start.1 = (bf16[128,16,128]{2,1,0:T(8,128)(2,1)S(1)}, bf16[128,16,128]{2,1,0:T(8,128)(2,1)S(1)}, u32[]{:S(2)}, u32[]{:S(2)}) collective-permute-start(bf16[128,16,128]{2,1,0:T(8,128)(2,1)S(1)} %get-tuple-element.39), channel_id=1, source_target_pairs={{0,1},{1,0},{2,3},{3,2},{4,5},{5,4},{6,7},{7,6},{8,9},{9,8},{10,11... | collective-permute-start | bytes 1572872 | tf_op jit(solution)/shard_map/ppermute | solution.py:313
  5.4 3.2 %collective-permute-start = (bf16[128,16,128]{2,1,0:T(8,128)(2,1)S(1)}, bf16[128,16,128]{2,1,0:T(8,128)(2,1)S(1)}, u32[]{:S(2)}, u32[]{:S(2)}) collective-permute-start(bf16[128,16,128]{2,1,0:T(8,128)(2,1)S(1)} %get-tuple-element.38), channel_id=1, source_target_pairs={{0,1},{1,0},{2,3},{3,2},{4,5},{5,4},{6,7},{7,6},{8,9},{9,8},{10,11... | collective-permute-start | bytes 1572872 | tf_op jit(solution)/shard_map/ppermute | solution.py:309
  5.5 29.8 %copy-start.1 = (f32[1,16]{1,0:T(1,128)S(1)}, f32[1,16]{1,0:T(1,128)}, u32[]{:S(2)}) copy-start(f32[1,16]{1,0:T(1,128)} %refs_9_.1) | copy-start | bytes 196
  8.9 8.8 %collective-permute-start.2 = (bf16[16,32,128]{2,1,0:T(8,128)(2,1)S(1)}, bf16[16,32,128]{2,1,0:T(8,128)(2,1)S(1)}, u32[]{:S(2)}, u32[]{:S(2)}) collective-permute-start(bf16[16,32,128]{2,1,0:T(8,128)(2,1)S(1)} %get-tuple-element.40), channel_id=1, source_target_pairs={{0,2},{2,0},{4,8},{6,10},{8,4},{10,6},{12,14},{14,12},{1,3},{3,1},... | collective-permute-start | bytes 393224 | tf_op jit(solution)/shard_map/ppermute | solution.py:489
  11.9 9.4 %collective-permute-start.3 = (bf16[16,32,128]{2,1,0:T(8,128)(2,1)S(1)}, bf16[16,32,128]{2,1,0:T(8,128)(2,1)S(1)}, u32[]{:S(2)}, u32[]{:S(2)}) collective-permute-start(bf16[16,32,128]{2,1,0:T(8,128)(2,1)S(1)} %get-tuple-element.41), channel_id=1, source_target_pairs={{0,4},{2,6},{4,0},{6,2},{8,12},{10,14},{12,8},{14,10},{1,5},{3,7},... | collective-permute-start | bytes 393224 | tf_op jit(solution)/shard_map/ppermute | solution.py:489
  13.6 12.9 %collective-permute-start.4 = (bf16[16,32,128]{2,1,0:T(8,128)(2,1)S(1)}, bf16[16,32,128]{2,1,0:T(8,128)(2,1)S(1)}, u32[]{:S(2)}, u32[]{:S(2)}) collective-permute-start(bf16[16,32,128]{2,1,0:T(8,128)(2,1)S(1)} %get-tuple-element.42), channel_id=1, source_target_pairs={{0,8},{2,10},{4,12},{6,14},{8,0},{10,2},{12,4},{14,6},{1,9},{3,11}... | collective-permute-start | bytes 393224 | tf_op jit(solution)/shard_map/ppermute | solution.py:489
  16.1 19.2 %collective-permute-start.5 = (bf16[16,32,128]{2,1,0:T(8,128)(2,1)S(1)}, bf16[16,32,128]{2,1,0:T(8,128)(2,1)S(1)}, u32[]{:S(2)}, u32[]{:S(2)}) collective-permute-start(bf16[16,32,128]{2,1,0:T(8,128)(2,1)S(1)} %get-tuple-element.43), channel_id=1, source_target_pairs={{0,10},{2,8},{4,14},{6,12},{8,2},{10,0},{12,6},{14,4},{1,11},{3,9}... | collective-permute-start | bytes 393224 | tf_op jit(solution)/shard_map/ppermute | solution.py:489
  17.4 17.9 %collective-permute-start.6 = (bf16[16,32,128]{2,1,0:T(8,128)(2,1)S(1)}, bf16[16,32,128]{2,1,0:T(8,128)(2,1)S(1)}, u32[]{:S(2)}, u32[]{:S(2)}) collective-permute-start(bf16[16,32,128]{2,1,0:T(8,128)(2,1)S(1)} %get-tuple-element.44), channel_id=1, source_target_pairs={{0,6},{2,4},{4,2},{6,0},{8,14},{10,12},{12,10},{14,8},{1,7},{3,5},... | collective-permute-start | bytes 393224 | tf_op jit(solution)/shard_map/ppermute | solution.py:489
  17.7 17.5 %collective-permute-start.7 = (bf16[16,32,128]{2,1,0:T(8,128)(2,1)S(1)}, bf16[16,32,128]{2,1,0:T(8,128)(2,1)S(1)}, u32[]{:S(2)}, u32[]{:S(2)}) collective-permute-start(bf16[16,32,128]{2,1,0:T(8,128)(2,1)S(1)} %get-tuple-element.45), channel_id=1, source_target_pairs={{0,14},{2,12},{4,10},{6,8},{8,6},{10,4},{12,2},{14,0},{1,15},{3,13... | collective-permute-start | bytes 393224 | tf_op jit(solution)/shard_map/ppermute | solution.py:489
  21.3 14.0 %collective-permute-start.8 = (bf16[16,32,128]{2,1,0:T(8,128)(2,1)S(1)}, bf16[16,32,128]{2,1,0:T(8,128)(2,1)S(1)}, u32[]{:S(2)}, u32[]{:S(2)}) collective-permute-start(bf16[16,32,128]{2,1,0:T(8,128)(2,1)S(1)} %get-tuple-element.46), channel_id=1, source_target_pairs={{0,12},{2,14},{4,6},{6,4},{8,10},{10,8},{12,0},{14,2},{1,13},{3,15... | collective-permute-start | bytes 393224 | tf_op jit(solution)/shard_map/ppermute | solution.py:489
